TPU v7x, 32 devices: a whole 2x2x4 slice. The times are simulated.
32 devices in a mesh: groups: 2 (over y), rowt: 4 (over z), colt: 2 (over x), site: 2 (over core).
Axes of the slice: x: 2, y: 2, z: 4, core: 2. Of those that a mesh axis runs over, the one named last changes fastest.
Arguments:
- seed_green: bfloat16 [8, 2, 768, 768], P(('groups', 'rowt'), 'colt', None, 'site'), parts along dimension 0, may hold values from -6 to 6
- field_spins: int32 [4, 8, 768], P(None, ('groups', 'rowt')), parts along dimension 1, may hold values from 0 to 1
- hop_matrix: float32 [768, 768], replicated, may hold values from -0.21875 to 0.21875
- vertex: bfloat16 [768, 768], replicated, may hold values from -0.21875 to 0.21875
Outputs:
- measured: bfloat16 [8, 2, 768, 768], P(('groups', 'rowt'), 'colt', None, 'site'), parts along dimension 0
There are 2 independent parts, one for each index of `groups`. A program takes and returns all parts, laid end to end along the dimension named above; an argument that names none is the same for every part. Nothing has to cross between parts.
All inputs are finite; a program needn't handle non-finite values.
Results may differ from a plain program's by a relative error of at most 0.0051.
Values may be sent and summed in bfloat16 or wider, within the bound.
A program may use at most 64 MiB of HBM per device.

v0:
```python
import jax
import jax.numpy as jnp
from jax import lax
from jax.sharding import PartitionSpec as P

coupling = 0.45
keep_share = 0.8
hop_share = 0.3


def partner(x, axis, distance):
    return lax.ppermute(x, axis, [(i, i ^ 1 << distance) for i in range(lax.axis_size(axis))])


def advance(current, hop_matrix, weights_row, sign_value):
    hopped = jnp.dot(hop_matrix, current, precision=lax.Precision.HIGHEST)
    image = keep_share * current + hop_share * hopped
    return (sign_value * weights_row)[:, None] * image


def measure(current, vertex):
    rounded = current.astype(jnp.bfloat16)
    top_bit = lax.axis_size(("colt", "site")).bit_length() - 2
    local_rows = lax.all_to_all(rounded, "site", split_axis=0, concat_axis=1, tiled=True)
    partner_rows = partner(local_rows, ("colt", "site"), top_bit)
    pair_product = (rounded.astype(jnp.float32) * partner_rows.T.astype(jnp.float32)).astype(
        jnp.bfloat16
    )
    return jnp.dot(vertex, pair_product, preferred_element_type=jnp.float32)


def per_device(seed_green, field_spins, hop_matrix, vertex):
    wraps = field_spins.shape[0]
    row_count = lax.axis_size("rowt")
    row_index = lax.axis_index("rowt")
    weights = jnp.exp(coupling * (2.0 * field_spins.astype(jnp.float32) - 1.0))
    current = seed_green[0, 0].astype(jnp.float32)
    all_weights = lax.all_gather(weights, "rowt", axis=1, tiled=True)
    measured = jnp.zeros_like(current)
    for wrap_step in range(wraps):
        target = (row_index + wrap_step + 1) % row_count
        weights_row = lax.dynamic_index_in_dim(all_weights[wrap_step], target, 0, keepdims=False)
        sign_value = jnp.where(target == 0, -1.0, 1.0).astype(jnp.float32)
        current = advance(current, hop_matrix, weights_row, sign_value)
        measured = measured + measure(current, vertex)
    result = (measured / wraps).astype(jnp.bfloat16)
    return result[None, None]


def solution(mesh):
    return jax.shard_map(
        per_device,
        mesh=mesh,
        in_specs=(
            P(("groups", "rowt"), "colt", None, "site"),
            P(None, ("groups", "rowt"), None),
            P(),
            P(),
        ),
        out_specs=P(("groups", "rowt"), "colt", None, "site"),
        check_vma=False,
    )
```

profile of v0, /device:TPU:0, one launch (start us, length us, event | category | flops | bytes accessed | tf_op | source)
XLA Modules:
  0.0 87.3 jit_solution(8937611655515566812)
XLA Ops:
  0.0 0.9 fusion.28
  0.9 14.7 %all_gather.3 = f32[4,4,768]{2,0,1:T(4,128)S(1)} all-gather(f32[4,1,768]{2,0,1:T(4,128)S(1)} %fusion.28), channel_id=1, replica_groups=mesh['groups'=2,'rowt'=4,'colt'=2,'site'=2] {'rowt'}, dimensions={1}, use_global_device_ids=true | all-gather | bytes 61440 | tf_op jit(solution)/shard_map/all_gather | solution.py:38
  15.7 3.3 %fusion.31 = (bf16[768,384]{1,0:T(8,128)(2,1)S(1)}, f32[768,384]{1,0:T(8,128)S(1)}) fusion(f32[768,768]{1,0:T(8,128)S(1)} %copy-done, bf16[1,1,768,384]{3,2,1,0:T(8,128)(2,1)} %param.4, f32[768]{0:T(1024)S(1)} %multiply_reduce_fusion.3), kind=kOutput, calls=%fused_computation.43 | convolution fusion | flops 2719678464 | bytes 4721664 | tf_op jit(solution)/shard_map/dot_general | solution.py:16
  19.1 5.0 %fusion.30 = (bf16[768,384]{1,0:T(8,128)(2,1)S(1)}, f32[768,384]{1,0:T(8,128)}) fusion(f32[768,384]{1,0:T(8,128)S(1)} %get-tuple-element.12, f32[768,768]{1,0:T(8,128)S(1)} %copy-done, f32[768]{0:T(1024)S(1)} %get-tuple-element.16), kind=kOutput, calls=%fused_computation.42 | convolution fusion | flops 2719383552 | bytes 5311488 | tf_op jit(solution)/shard_map/dot_general | solution.py:16
  24.1 0.8 copy-done.4
  24.9 4.2 %all_to_all.76 = bf16[2,384,384]{2,1,0:T(8,128)(2,1)S(1)} all-to-all(bf16[2,384,384]{2,1,0:T(8,128)(2,1)S(1)} %bitcast.73), channel_id=1, replica_groups=mesh['groups'=2,'rowt'=4,'colt'=2,'site'=2] {'site'}, dimensions={0} | all-to-all | bytes 1179648 | tf_op jit(solution)/shard_map/all_to_all | solution.py:24
  29.1 1.1 %copy.16 = bf16[384,2,384]{0,2,1:T(8,128)(2,1)} copy(bf16[384,2,384]{2,0,1:T(8,128)(2,1)S(1)} %bitcast.76) | data formatting | bytes 1179648 | tf_op jit(solution)/shard_map/all_to_all | solution.py:24
  30.1 1.5 %collective-permute-start.1 = (bf16[384,768]{0,1:T(8,128)(2,1)}, bf16[384,768]{0,1:T(8,128)(2,1)}, u32[]{:S(2)}, u32[]{:S(2)}) collective-permute-start(bf16[384,768]{0,1:T(8,128)(2,1)} %bitcast.80), channel_id=1, source_target_pairs={{0,2},{1,3},{2,0},{3,1},{4,6},{5,7},{6,4},{7,5},{8,10},{9,11},{10,... | collective-permute-start | bytes 1769480 | tf_op jit(solution)/shard_map/ppermute | solution.py:12
  31.6 4.2 %all_to_all.77 = bf16[2,384,384]{2,1,0:T(8,128)(2,1)S(1)} all-to-all(bf16[2,384,384]{2,1,0:T(8,128)(2,1)S(1)} %bitcast.74), channel_id=1, replica_groups=mesh['groups'=2,'rowt'=4,'colt'=2,'site'=2] {'site'}, dimensions={0} | all-to-all | bytes 1179648 | tf_op jit(solution)/shard_map/all_to_all | solution.py:24
  35.8 1.1 %copy.14 = bf16[384,2,384]{0,2,1:T(8,128)(2,1)} copy(bf16[384,2,384]{2,0,1:T(8,128)(2,1)S(1)} %bitcast.77) | data formatting | bytes 1179648 | tf_op jit(solution)/shard_map/all_to_all | solution.py:24
  36.9 0.5 collective-permute-start
  37.4 5.6 %fusion.32 = (bf16[768,384]{1,0:T(8,128)(2,1)S(1)}, f32[768,384]{1,0:T(8,128)S(1)}) fusion(f32[768,384]{1,0:T(8,128)} %get-tuple-element.10, f32[768,768]{1,0:T(8,128)S(1)} %copy-done, f32[768]{0:T(1024)S(1)} %get-tuple-element.15), kind=kOutput, calls=%fused_computation.44 | convolution fusion | flops 2719383552 | bytes 5311488 | tf_op jit(solution)/shard_map/dot_general | solution.py:16
  43.1 0.8 copy-done.2
  43.9 4.9 %all_to_all.78 = bf16[2,384,384]{2,1,0:T(8,128)(2,1)} all-to-all(bf16[2,384,384]{2,1,0:T(8,128)(2,1)S(1)} %bitcast.72), channel_id=1, replica_groups=mesh['groups'=2,'rowt'=4,'colt'=2,'site'=2] {'site'}, dimensions={0} | all-to-all | bytes 1179648 | tf_op jit(solution)/shard_map/all_to_all | solution.py:24
  48.8 2.1 %copy.18 = bf16[384,2,384]{0,2,1:T(8,128)(2,1)} copy(bf16[384,2,384]{2,0,1:T(8,128)(2,1)} %bitcast.78) | data formatting | bytes 1179648 | tf_op jit(solution)/shard_map/all_to_all | solution.py:24
  50.9 1.5 %collective-permute-start.2 = (bf16[384,768]{0,1:T(8,128)(2,1)}, bf16[384,768]{0,1:T(8,128)(2,1)}, u32[]{:S(2)}, u32[]{:S(2)}) collective-permute-start(bf16[384,768]{0,1:T(8,128)(2,1)} %bitcast.81), channel_id=1, source_target_pairs={{0,2},{1,3},{2,0},{3,1},{4,6},{5,7},{6,4},{7,5},{8,10},{9,11},{10,... | collective-permute-start | bytes 1769480 | tf_op jit(solution)/shard_map/ppermute | solution.py:12
  52.5 3.9 %fusion.12 = bf16[768,384]{1,0:T(8,128)(2,1)S(1)} fusion(f32[768,384]{1,0:T(8,128)S(1)} %get-tuple-element.14, f32[768,768]{1,0:T(8,128)S(1)} %copy-done, f32[768]{0:T(1024)S(1)} %multiply_reduce_fusion), kind=kOutput, calls=%fused_computation.19 | convolution fusion | flops 2719383552 | bytes 4131840 | tf_op jit(solution)/shard_map/dot_general | solution.py:16
  56.4 0.8 copy-done.7
  57.2 5.1 %all_to_all.79 = bf16[2,384,384]{2,1,0:T(8,128)(2,1)} all-to-all(bf16[2,384,384]{2,1,0:T(8,128)(2,1)S(1)} %bitcast.75), channel_id=1, replica_groups=mesh['groups'=2,'rowt'=4,'colt'=2,'site'=2] {'site'}, dimensions={0} | all-to-all | bytes 1179648 | tf_op jit(solution)/shard_map/all_to_all | solution.py:24
  62.3 2.2 %copy.20 = bf16[384,2,384]{0,2,1:T(8,128)(2,1)} copy(bf16[384,2,384]{2,0,1:T(8,128)(2,1)} %bitcast.79) | data formatting | bytes 1179648 | tf_op jit(solution)/shard_map/all_to_all | solution.py:24
  64.4 0.5 collective-permute-start.3
  65.0 0.0 collective-permute-done.1
  65.0 1.9 %fusion.20 = f32[384,768]{1,0:T(8,128)S(1)} fusion(bf16[768,768]{1,0:T(8,128)(2,1)S(1)} %copy-done.1, bf16[384,768]{0,1:T(8,128)(2,1)} %collective-permute-done.1, bf16[768,384]{1,0:T(8,128)(2,1)} %copy-done.4), kind=kOutput, calls=%fused_computation.30 | convolution fusion | flops 454164480 | bytes 3538944 | tf_op jit(solution)/shard_map/dot_general | solution.py:29
  66.9 0.0 copy-start.3
  66.9 0.0 collective-permute-done
  66.9 1.8 %convolution_add_fusion.2 = f32[384,768]{1,0:T(8,128)S(1)} fusion(f32[384,768]{1,0:T(8,128)S(1)} %fusion.20, bf16[768,768]{1,0:T(8,128)(2,1)S(1)} %copy-done.1, bf16[384,768]{0,1:T(8,128)(2,1)} %collective-permute-done, bf16[768,384]{1,0:T(8,128)(2,1)S(1)} %copy-done.6), kind=kOutput, calls=%fused_computation.6 | convolution fusion | flops 454459392 | bytes 4718592 | tf_op jit(solution)/shard_map/dot_general | solution.py:29
  68.8 0.0 copy-start.8
  68.8 3.1 %collective-permute-done.2 = bf16[384,768]{0,1:T(8,128)(2,1)} collective-permute-done((bf16[384,768]{0,1:T(8,128)(2,1)}, bf16[384,768]{0,1:T(8,128)(2,1)}, u32[]{:S(2)}, u32[]{:S(2)}) %collective-permute-start.2) | collective-permute-done | bytes 589856 | tf_op jit(solution)/shard_map/ppermute | solution.py:12
  71.9 1.8 %convolution_add_fusion.1 = f32[384,768]{1,0:T(8,128)S(1)} fusion(f32[384,768]{1,0:T(8,128)S(1)} %convolution_add_fusion.2, bf16[768,768]{1,0:T(8,128)(2,1)S(1)} %copy-done.1, bf16[384,768]{0,1:T(8,128)(2,1)} %collective-permute-done.2, bf16[768,384]{1,0:T(8,128)(2,1)S(1)} %copy-done.3), kind=kOutput, calls=%fused_computation.3 | convolution fusion | flops 454459392 | bytes 4718592 | tf_op jit(solution)/shard_map/dot_general | solution.py:29
  73.7 10.0 %collective-permute-done.3 = bf16[384,768]{0,1:T(8,128)(2,1)S(1)} collective-permute-done((bf16[384,768]{0,1:T(8,128)(2,1)}, bf16[384,768]{0,1:T(8,128)(2,1)S(1)}, u32[]{:S(2)}, u32[]{:S(2)}) %collective-permute-start.3) | collective-permute-done | bytes 589856 | tf_op jit(solution)/shard_map/ppermute | solution.py:12
  83.6 1.5 %fusion.14 = bf16[1,1,768,384]{2,3,1,0:T(8,128)(2,1)} fusion(f32[384,768]{1,0:T(8,128)S(1)} %convolution_add_fusion.1, bf16[768,768]{1,0:T(8,128)(2,1)S(1)} %copy-done.1, bf16[384,768]{0,1:T(8,128)(2,1)S(1)} %collective-permute-done.3, bf16[768,384]{1,0:T(8,128)(2,1)S(1)} %copy-done.8), kind=kOutput, calls=%fused_computation.21 | convolution fusion | flops 455049216 | bytes 4128768 | tf_op jit(solution)/shard_map/dot_general | solution.py:29
  85.2 2.1 %copy.21 = bf16[1,1,768,384]{3,2,1,0:T(8,128)(2,1)} copy(bf16[1,1,768,384]{2,3,1,0:T(8,128)(2,1)} %fusion.14) | data formatting | bytes 1179648 | tf_op jit(solution)/shard_map/broadcast_in_dim | solution.py:47
  (17 shorter events, 0.1 us)
Async XLA Ops:
  0.0 15.7 %copy-start = (f32[768,768]{1,0:T(8,128)S(1)}, f32[768,768]{1,0:T(8,128)}, u32[]{:S(2)}) copy-start(f32[768,768]{1,0:T(8,128)} %param.6) | copy-start | bytes 7077892
  19.0 12.6 %copy-start.5 = (bf16[768,384]{1,0:T(8,128)(2,1)}, bf16[768,384]{1,0:T(8,128)(2,1)S(1)}, u32[]{:S(2)}) copy-start(bf16[768,384]{1,0:T(8,128)(2,1)S(1)} %get-tuple-element.11) | copy-start | bytes 1769476
  24.1 0.8 copy-start.4
  30.1 34.9 %collective-permute-start.1 = (bf16[384,768]{0,1:T(8,128)(2,1)}, bf16[384,768]{0,1:T(8,128)(2,1)}, u32[]{:S(2)}, u32[]{:S(2)}) collective-permute-start(bf16[384,768]{0,1:T(8,128)(2,1)} %bitcast.80), channel_id=1, source_target_pairs={{0,2},{1,3},{2,0},{3,1},{4,6},{5,7},{6,4},{7,5},{8,10},{9,11},{10,... | collective-permute-start | bytes 1769480 | tf_op jit(solution)/shard_map/ppermute | solution.py:12
  36.9 30.0 %collective-permute-start = (bf16[384,768]{0,1:T(8,128)(2,1)}, bf16[384,768]{0,1:T(8,128)(2,1)}, u32[]{:S(2)}, u32[]{:S(2)}) collective-permute-start(bf16[384,768]{0,1:T(8,128)(2,1)} %bitcast.3), channel_id=1, source_target_pairs={{0,2},{1,3},{2,0},{3,1},{4,6},{5,7},{6,4},{7,5},{8,10},{9,11},{10,... | collective-permute-start | bytes 1769480 | tf_op jit(solution)/shard_map/ppermute | solution.py:12
  43.0 0.8 copy-start.2
  50.9 21.0 %collective-permute-start.2 = (bf16[384,768]{0,1:T(8,128)(2,1)}, bf16[384,768]{0,1:T(8,128)(2,1)}, u32[]{:S(2)}, u32[]{:S(2)}) collective-permute-start(bf16[384,768]{0,1:T(8,128)(2,1)} %bitcast.81), channel_id=1, source_target_pairs={{0,2},{1,3},{2,0},{3,1},{4,6},{5,7},{6,4},{7,5},{8,10},{9,11},{10,... | collective-permute-start | bytes 1769480 | tf_op jit(solution)/shard_map/ppermute | solution.py:12
  56.4 0.8 copy-start.7
  57.2 7.8 %copy-start.1 = (bf16[768,768]{1,0:T(8,128)(2,1)S(1)}, bf16[768,768]{1,0:T(8,128)(2,1)}, u32[]{:S(2)}) copy-start(bf16[768,768]{1,0:T(8,128)(2,1)} %param.7) | copy-start | bytes 3538948
  64.4 2.5 %copy-start.6 = (bf16[768,384]{1,0:T(8,128)(2,1)S(1)}, bf16[768,384]{1,0:T(8,128)(2,1)}, u32[]{:S(2)}) copy-start(bf16[768,384]{1,0:T(8,128)(2,1)} %copy-done.5) | copy-start | bytes 1769476
  64.4 19.2 %collective-permute-start.3 = (bf16[384,768]{0,1:T(8,128)(2,1)}, bf16[384,768]{0,1:T(8,128)(2,1)S(1)}, u32[]{:S(2)}, u32[]{:S(2)}) collective-permute-start(bf16[384,768]{0,1:T(8,128)(2,1)} %bitcast.82), channel_id=1, source_target_pairs={{0,2},{1,3},{2,0},{3,1},{4,6},{5,7},{6,4},{7,5},{8,10},{9,11},{10,... | collective-permute-start | bytes 1769480 | tf_op jit(solution)/shard_map/ppermute | solution.py:12
  66.9 5.0 %copy-start.3 = (bf16[768,384]{1,0:T(8,128)(2,1)S(1)}, bf16[768,384]{1,0:T(8,128)(2,1)}, u32[]{:S(2)}) copy-start(bf16[768,384]{1,0:T(8,128)(2,1)} %copy-done.2) | copy-start | bytes 1769476
  68.8 14.9 %copy-start.8 = (bf16[768,384]{1,0:T(8,128)(2,1)S(1)}, bf16[768,384]{1,0:T(8,128)(2,1)}, u32[]{:S(2)}) copy-start(bf16[768,384]{1,0:T(8,128)(2,1)} %copy-done.7) | copy-start | bytes 1769476
where the time goes:
time: 87.9 us; the launch traced here: 87.3 us
  blocking collectives  33.2 us (38%)
  matrix products  24.8 us (28%)
  waiting for transfers between devices  13.1 us (15%)
  local copies, waits for them, and re-layouts  11.1 us (13%)
  starting transfers between devices  4.05 us (5%)
  other arithmetic  0.94 us (1%)
    all_to_all x4, blocking collectives, measure(): lax.all_to_all(rounded, 'site', split_axis=0, concat_axis=1, tiled=True)  18.4 us
    dot_general x4, matrix products, advance(): hopped = jnp.dot(hop_matrix, current, precision=lax.Precision.HIGHEST)  17.8 us
    all_gather x1, blocking collectives, per_device(): all_weights = lax.all_gather(weights, 'rowt', axis=1, tiled=True)  14.7 us
    ppermute x4, waiting for transfers between devices, partner(): lax.ppermute(x, axis, [(i, i ^ 1 << distance) for i in range(lax.axis_siz...  13.1 us
    dot_general x4, matrix products, measure(): return jnp.dot(vertex, pair_product, preferred_element_type=jnp.float32)  7.01 us
    all_to_all x4, local copies, waits for them, and re-layouts, measure(): lax.all_to_all(rounded, 'site', split_axis=0, concat_axis=1, tiled=True)  6.42 us
    ppermute x4, starting transfers between devices, partner(): lax.ppermute(x, axis, [(i, i ^ 1 << distance) for i in range(lax.axis_siz...  4.05 us
    unnamed x18, local copies, waits for them, and re-layouts  2.48 us
  transfers between devices with their start and end apart: 4, of which 2 were waited for; matrix products, arithmetic and copies ran while one was open for 23% of the time, Pallas kernels for 0%

commit v1 on v0

v1 whole, which is shorter than its diff:
```python
import functools

import jax
import jax.numpy as jnp
from jax import lax
from jax.experimental import pallas as pl
from jax.experimental.pallas import tpu as pltpu
from jax.sharding import PartitionSpec as P

coupling = 0.45
keep_share = 0.8
hop_share = 0.3
MESH = pl.DeviceIdType.MESH
F32 = jnp.float32
BF16 = jnp.bfloat16


def split(x):
    high = x.astype(BF16)
    return high, (x - high.astype(F32)).astype(BF16)


def nn(a, b):
    return lax.dot_general(a, b, (((1,), (0,)), ((), ())), preferred_element_type=F32)


def nt(a, b):
    return lax.dot_general(a, b, (((1,), (1,)), ((), ())), preferred_element_type=F32)


def chunk_list(columns):
    chunks, start = [], 0
    while start < columns:
        width = min(256, columns - start)
        chunks.append((start, width))
        start += width
    return chunks


def kernel(
    rows_n, cols_n,
    seed, spins, hop, vertex, out,
    own, hop_v, vertex_v, spin_v, theirs, a_hi, a_lo, x_hi, x_lo, y_hi, y_lo, cross, t_hi, t_lo,
    local_sem, seed_send, seed_recv, spin_send, spin_recv, cross_send, cross_recv,
):
    order, columns = own.shape
    wraps = spins.shape[0]
    row = lax.axis_index("rowt")
    col = lax.axis_index("colt")
    site = lax.axis_index("site")
    other_site = 1 - site
    other_col = lax.rem(col + cols_n // 2, cols_n)
    chunks = chunk_list(columns)

    local = [
        pltpu.make_async_copy(seed.at[0, 0], own, local_sem.at[0]),
        pltpu.make_async_copy(hop, hop_v, local_sem.at[1]),
        pltpu.make_async_copy(vertex, vertex_v, local_sem.at[2]),
    ]
    for copy in local:
        copy.start()

    distances = sorted({(w + 1) % rows_n for w in range(wraps)} - {0})
    peers = sorted(set(distances) | {(-d) % rows_n for d in distances})
    barrier = pltpu.get_barrier_semaphore()
    for peer in peers:
        pl.semaphore_signal(
            barrier, inc=1, device_id={"rowt": lax.rem(row + peer, rows_n)}, device_id_type=MESH
        )
    pl.semaphore_signal(barrier, inc=1, device_id={"colt": other_col}, device_id_type=MESH)
    pl.semaphore_signal(barrier, inc=1, device_id={"site": other_site}, device_id_type=MESH)
    pl.semaphore_wait(barrier, len(peers) + 2)

    spin_copies = []
    for w in range(wraps):
        distance = (w + 1) % rows_n
        if distance == 0:
            copy = pltpu.make_async_copy(spins.at[w], spin_v.at[w], spin_recv.at[w])
        else:
            copy = pltpu.make_async_remote_copy(
                src_ref=spins.at[w],
                dst_ref=spin_v.at[w],
                send_sem=spin_send.at[w],
                recv_sem=spin_recv.at[w],
                device_id={"rowt": lax.rem(row + rows_n - distance, rows_n)},
                device_id_type=MESH,
            )
        copy.start()
        spin_copies.append(copy)
    seed_copies = []
    for c, (start, width) in enumerate(chunks):
        copy = pltpu.make_async_remote_copy(
            src_ref=seed.at[0, 0, :, pl.ds(start, width)],
            dst_ref=theirs.at[:, pl.ds(start, width)],
            send_sem=seed_send.at[c],
            recv_sem=seed_recv.at[c],
            device_id={"colt": other_col},
            device_id_type=MESH,
        )
        copy.start()
        seed_copies.append(copy)

    local[1].wait()
    step = 128
    for r in range(0, order, step):
        a = hop_share * hop_v[r:r + step, :]
        diagonal = lax.broadcasted_iota(jnp.int32, a.shape, 0) + r == lax.broadcasted_iota(
            jnp.int32, a.shape, 1
        )
        high, low = split(a + jnp.where(diagonal, F32(keep_share), F32(0)))
        a_hi[r:r + step, :] = high
        a_lo[r:r + step, :] = low

    local[0].wait()
    x0 = own[...].T

    def weight_row(w):
        sign = jnp.where(lax.rem(row + w + 1, rows_n) == 0, F32(-1), F32(1))
        return sign * jnp.exp(coupling * (2.0 * spin_v[w].astype(F32) - 1.0))

    tile = 256
    weights_col = []
    for w in range(wraps):
        for n in range(0, order, tile):
            high = a_hi[n:n + tile, :]
            low = a_lo[n:n + tile, :]
            if w == 0:
                product = nt(x0, high) + nt(x0, low)
            else:
                before = x_hi[w - 1]
                product = nt(before, high) + nt(before, low) + nt(x_lo[(w - 1) % 2], high)
            if n == 0:
                spin_copies[w].wait()
                weights = weight_row(w)
                weights_col.append(jnp.broadcast_to(weights, (128, order)).T)
            high, low = split(product * weights[:, n:n + tile])
            x_hi[w, :, n:n + tile] = high
            if w < wraps - 1:
                x_lo[w % 2, :, n:n + tile] = low

    row_of_other = pl.ds(pl.multiple_of(other_site * columns, columns), columns)
    row_of_own = pl.ds(pl.multiple_of(site * columns, columns), columns)
    cross_copies = []
    for c, (start, width) in enumerate(chunks):
        seed_copies[c].wait_recv()
        part = pl.ds(start, width)
        for w in range(wraps):
            if w == 0:
                before = theirs[:, start:start + width]
                product = nn(a_hi[...], before) + nn(a_lo[...], before)
            else:
                before = y_hi[w - 1, :, start:start + width]
                product = (
                    nn(a_hi[...], before) + nn(a_lo[...], before)
                    + nn(a_hi[...], y_lo[:, :width])
                )
            scale = jnp.concatenate([weights_col[w]] * (width // 128), axis=1)
            high, low = split(product * scale)
            y_hi[w, :, start:start + width] = high
            if w < wraps - 1:
                y_lo[:, :width] = low
            copy = pltpu.make_async_remote_copy(
                src_ref=y_hi.at[w, row_of_other, part],
                dst_ref=cross.at[w, :, part],
                send_sem=cross_send.at[c, w],
                recv_sem=cross_recv.at[c, w],
                device_id={"site": other_site},
                device_id_type=MESH,
            )
            copy.start()
            cross_copies.append(copy)

    def pair_sum(near, far):
        total = None
        for w in range(wraps):
            pair = (near(w).astype(F32) * far(w).astype(F32)).astype(BF16).astype(F32)
            total = pair if total is None else total + pair
        return split(total)

    own_lanes = pl.ds(pl.multiple_of(site * columns, columns), columns)
    other_lanes = pl.ds(pl.multiple_of(other_site * columns, columns), columns)
    high, low = pair_sum(lambda w: x_hi[w, :, own_lanes], lambda w: y_hi[w, row_of_own, :])
    t_hi[:, own_lanes] = high
    t_lo[:, own_lanes] = low
    for copy in cross_copies:
        copy.wait_recv()
    high, low = pair_sum(lambda w: x_hi[w, :, other_lanes], lambda w: cross[w])
    t_hi[:, other_lanes] = high
    t_lo[:, other_lanes] = low

    local[2].wait()
    for m in range(0, order, tile):
        v = vertex_v[m:m + tile, :]
        out[0, 0, m:m + tile, :] = ((nt(v, t_hi[...]) + nt(v, t_lo[...])) / wraps).astype(BF16)

    for copy in seed_copies + cross_copies:
        copy.wait_send()


def per_device(rows_n, cols_n, seed_green, field_spins, hop_matrix, vertex):
    wraps = field_spins.shape[0]
    order, columns = seed_green.shape[2:]
    n_chunks = len(chunk_list(columns))
    dma = pltpu.SemaphoreType.DMA
    any_space = pl.BlockSpec(memory_space=pl.ANY)
    return pl.pallas_call(
        functools.partial(kernel, rows_n, cols_n),
        out_shape=jax.ShapeDtypeStruct(seed_green.shape, BF16),
        in_specs=[any_space] * 4,
        out_specs=pl.BlockSpec(memory_space=pltpu.VMEM),
        scratch_shapes=[
            pltpu.VMEM((order, columns), BF16),
            pltpu.VMEM((order, order), F32),
            pltpu.VMEM((order, order), BF16),
            pltpu.VMEM((wraps, 1, order), jnp.int32),
            pltpu.VMEM((order, columns), BF16),
            pltpu.VMEM((order, order), BF16),
            pltpu.VMEM((order, order), BF16),
            pltpu.VMEM((wraps, columns, order), BF16),
            pltpu.VMEM((2, columns, order), BF16),
            pltpu.VMEM((wraps, order, columns), BF16),
            pltpu.VMEM((order, 256), BF16),
            pltpu.VMEM((wraps, columns, columns), BF16),
            pltpu.VMEM((columns, order), BF16),
            pltpu.VMEM((columns, order), BF16),
            dma((3,)),
            dma((n_chunks,)),
            dma((n_chunks,)),
            dma((wraps,)),
            dma((wraps,)),
            dma((n_chunks, wraps)),
            dma((n_chunks, wraps)),
        ],
        compiler_params=pltpu.CompilerParams(
            collective_id=0, has_side_effects=True, vmem_limit_bytes=62 * 1024 * 1024
        ),
    )(seed_green, field_spins, hop_matrix, vertex)


def solution(mesh):
    body = functools.partial(per_device, mesh.shape["rowt"], mesh.shape["colt"])
    return jax.shard_map(
        body,
        mesh=mesh,
        in_specs=(
            P(("groups", "rowt"), "colt", None, "site"),
            P(None, ("groups", "rowt"), None),
            P(),
            P(),
        ),
        out_specs=P(("groups", "rowt"), "colt", None, "site"),
        check_vma=False,
    )
```

time: 87.9 us -> 38 us (0.43)
  Pallas kernels: 0 us -> 35.9 us
  blocking collectives: 33.2 us -> 0 us
  matrix products: 24.8 us -> 0 us
  waiting for transfers between devices: 13.1 us -> 0 us
  local copies, waits for them, and re-layouts: 11.1 us -> 1.94 us
  starting transfers between devices: 4.05 us -> 0 us
  other arithmetic: 0.94 us -> 0 us
    pallas_call x0 -> x1, Pallas kernels: none -> 35.9 us  [per_device(): pl.pallas_call(functools.partial(kernel, rows_n, cols_n), out_shape=jax.S...]
    dot_general x8 -> x0, matrix products: 24.8 us -> none  [the longest x4 17.8 us: advance(): hopped = jnp.dot(hop_matrix, current, precision=lax.Precision.HIGHEST)]
    all_to_all x4 -> x0, blocking collectives: 18.4 us -> none  [measure(): lax.all_to_all(rounded, 'site', split_axis=0, concat_axis=1, tiled=True)]
    all_gather x1 -> x0, blocking collectives: 14.7 us -> none  [per_device(): all_weights = lax.all_gather(weights, 'rowt', axis=1, tiled=True)]
    ppermute x4 -> x0, waiting for transfers between devices: 13.1 us -> none  [partner(): lax.ppermute(x, axis, [(i, i ^ 1 << distance) for i in range(lax.axis_siz...]
    all_to_all x4 -> x0, local copies, waits for them, and re-layouts: 6.42 us -> none  [measure(): lax.all_to_all(rounded, 'site', split_axis=0, concat_axis=1, tiled=True)]
    ppermute x4 -> x0, starting transfers between devices: 4.05 us -> none  [partner(): lax.ppermute(x, axis, [(i, i ^ 1 << distance) for i in range(lax.axis_siz...]
    broadcast_in_dim x1 -> x0, local copies, waits for them, and re-layouts: 2.12 us -> none  [per_device(): return result[None, None]]
  transfers between devices with their start and end apart: 4 -> 0, of which waited for: 2 -> 0; matrix products, arithmetic and copies ran while one was open for 23% -> 0% of each run, Pallas kernels for 0% -> 0%
where the time goes in v1:
time: 38 us; the launch traced here: 37.8 us
  Pallas kernels  35.9 us (94%)
  local copies, waits for them, and re-layouts  1.94 us (5%)
    pallas_call x1, Pallas kernels, per_device(): pl.pallas_call(functools.partial(kernel, rows_n, cols_n), out_shape=jax.S...  35.9 us
    unnamed x1, local copies, waits for them, and re-layouts  1.94 us

profile of v1, /device:TPU:0, one launch (start us, length us, event | category | flops | bytes accessed | tf_op | source)
XLA Modules:
  0.0 37.8 jit_solution(11903569264128202124)
XLA Ops:
  0.0 35.9 %shard_map.46 = bf16[1,1,768,384]{3,2,1,0:T(8,128)(2,1)} custom-call(bf16[1,1,768,384]{3,2,1,0:T(8,128)(2,1)} %seed.1, s32[4,1,768]{2,1,0:T(1,128)} %spins.1, f32[768,768]{1,0:T(8,128)} %hop.1, bf16[768,768]{1,0:T(8,128)(2,1)} %vertex.1), custom_call_target="tpu_custom_call" | custom-call | tf_op jit(solution)/shard_map/pallas_call | solution.py:206
  35.9 1.9 %copy.6 = bf16[1,1,768,384]{3,2,1,0:T(8,128)(2,1)} copy(bf16[1,1,768,384]{3,2,1,0:T(8,128)(2,1)} %shard_map.46) | data formatting | bytes 1179648

commit v2 on v1

v2 whole, which is shorter than its diff:
```python
import functools

import jax
import jax.numpy as jnp
from jax import lax
from jax.experimental import pallas as pl
from jax.experimental.pallas import tpu as pltpu
from jax.sharding import PartitionSpec as P

coupling = 0.45
keep_share = 0.8
hop_share = 0.3
MESH = pl.DeviceIdType.MESH
F32 = jnp.float32
BF16 = jnp.bfloat16


def split(x):
    high = x.astype(BF16)
    return high, (x - high.astype(F32)).astype(BF16)


def nn(a, b):
    return lax.dot_general(a, b, (((1,), (0,)), ((), ())), preferred_element_type=F32)


def nt(a, b):
    return lax.dot_general(a, b, (((1,), (1,)), ((), ())), preferred_element_type=F32)


def kernel(
    rows_n, cols_n,
    seed, spins, hop, vertex, out,
    own, hop_v, vertex_v, spin_v, theirs, a_hi, a_lo, x_hi, x_lo, y_hi, y_lo, m_hi, m_lo, total_v,
    local_sem, seed_send, seed_recv, pass_send, pass_recv, spin_send, spin_recv, cross_send,
    cross_recv,
):
    order, columns = own.shape
    wraps = spins.shape[0]
    row = lax.axis_index("rowt")
    col = lax.axis_index("colt")
    site = lax.axis_index("site")
    other_site = 1 - site
    other_col = lax.rem(col + cols_n // 2, cols_n)
    lanes = 128
    chunks = columns // lanes
    own_lanes = pl.ds(pl.multiple_of(site * columns, lanes), columns)
    row_of_other = pl.ds(pl.multiple_of(other_site * columns, lanes), columns)
    row_of_own = pl.ds(pl.multiple_of(site * columns, lanes), columns)

    local = [
        pltpu.make_async_copy(seed.at[0, 0], own, local_sem.at[0]),
        pltpu.make_async_copy(hop, hop_v, local_sem.at[1]),
        pltpu.make_async_copy(vertex, vertex_v, local_sem.at[2]),
    ]
    for copy in local:
        copy.start()

    distances = sorted({(w + 1) % rows_n for w in range(wraps)} - {0})
    peers = sorted(set(distances) | {(-d) % rows_n for d in distances})
    barrier = pltpu.get_barrier_semaphore()
    for peer in peers:
        pl.semaphore_signal(
            barrier, inc=1, device_id={"rowt": lax.rem(row + peer, rows_n)}, device_id_type=MESH
        )
    pl.semaphore_signal(barrier, inc=1, device_id={"colt": other_col}, device_id_type=MESH)
    pl.semaphore_signal(barrier, inc=1, device_id={"site": other_site}, device_id_type=MESH)
    pl.semaphore_wait(barrier, len(peers) + 2)

    spin_copies = []
    for w in range(wraps):
        distance = (w + 1) % rows_n
        if distance == 0:
            copy = pltpu.make_async_copy(spins.at[w], spin_v.at[w], spin_recv.at[w])
        else:
            copy = pltpu.make_async_remote_copy(
                src_ref=spins.at[w],
                dst_ref=spin_v.at[w],
                send_sem=spin_send.at[w],
                recv_sem=spin_recv.at[w],
                device_id={"rowt": lax.rem(row + rows_n - distance, rows_n)},
                device_id_type=MESH,
            )
        copy.start()
        spin_copies.append(copy)
    seed_copies, pass_copies = [], []
    for c in range(chunks):
        spot = pl.ds(pl.multiple_of(site * columns + c * lanes, lanes), lanes)
        seed_copies.append(pltpu.make_async_remote_copy(
            src_ref=seed.at[0, 0, :, pl.ds(c * lanes, lanes)],
            dst_ref=theirs.at[:, spot],
            send_sem=seed_send.at[c],
            recv_sem=seed_recv.at[c],
            device_id={"colt": other_col},
            device_id_type=MESH,
        ))
        pass_copies.append(pltpu.make_async_remote_copy(
            src_ref=theirs.at[:, spot],
            dst_ref=theirs.at[:, spot],
            send_sem=pass_send.at[c],
            recv_sem=pass_recv.at[c],
            device_id={"site": other_site},
            device_id_type=MESH,
        ))
        seed_copies[c].start()

    def pass_on(c):
        seed_copies[c].wait_recv()
        pass_copies[c].start()

    local[1].wait()
    step = 128
    for r in range(0, order, step):
        a = hop_share * hop_v[r:r + step, :]
        diagonal = lax.broadcasted_iota(jnp.int32, a.shape, 0) + r == lax.broadcasted_iota(
            jnp.int32, a.shape, 1
        )
        high, low = split(a + jnp.where(diagonal, F32(keep_share), F32(0)))
        a_hi[r:r + step, :] = high
        a_lo[r:r + step, :] = low

    local[0].wait()
    x0 = own[...].T

    def weight_row(w):
        sign = jnp.where(lax.rem(row + w + 1, rows_n) == 0, F32(-1), F32(1))
        return sign * jnp.exp(coupling * (2.0 * spin_v[w].astype(F32) - 1.0))

    tile = 256
    cross_copies = []
    for w in range(wraps):
        products = []
        for n in range(0, order, tile):
            high = a_hi[n:n + tile, :]
            low = a_lo[n:n + tile, :]
            if w == 0:
                product = nt(x0, high) + nt(x0, low)
            else:
                before = x_hi[w - 1]
                product = nt(before, high) + nt(before, low) + nt(x_lo[(w - 1) % 2], high)
            if n == 0:
                spin_copies[w].wait()
                weights = weight_row(w)
            high, low = split(product * weights[:, n:n + tile])
            x_hi[w, :, n:n + tile] = high
            if w < wraps - 1:
                x_lo[w % 2, :, n:n + tile] = low
        if w == 0:
            product = a_hi[:, own_lanes].astype(F32) + a_lo[:, own_lanes].astype(F32)
        else:
            product = (
                nn(a_hi[...], y_hi[w - 1]) + nn(a_lo[...], y_hi[w - 1])
                + nn(a_hi[...], y_lo[w - 1])
            )
        column = jnp.broadcast_to(weights, (lanes, order)).T
        high, low = split(product * jnp.concatenate([column] * chunks, axis=1))
        for part, (value, held, whole) in enumerate(((high, y_hi, m_hi), (low, y_lo, m_lo))):
            held[w] = value
            copy = pltpu.make_async_remote_copy(
                src_ref=held.at[w, row_of_other],
                dst_ref=whole.at[w, :, own_lanes],
                send_sem=cross_send.at[part, w],
                recv_sem=cross_recv.at[part, w],
                device_id={"site": other_site},
                device_id_type=MESH,
            )
            copy.start()
            cross_copies.append(copy)
            whole[w, :, own_lanes] = held[w, row_of_own]
        if w == wraps - 2:
            pass_on(0)

    def both(c):
        return [s * columns + c * lanes for s in range(2)]

    def take(ref, index, c):
        return jnp.concatenate([ref[index + (slice(a, a + lanes),)] for a in both(c)], axis=1)

    def pair_sum(c):
        pass_copies[c].wait_recv()
        block = take(theirs, (slice(None),), c)
        total = None
        for w in range(wraps):
            far = (nn(m_hi[w], block) + nn(m_lo[w], block)).astype(BF16)
            near = take(x_hi, (w, slice(None)), c)
            pair = (near.astype(F32) * far.astype(F32)).astype(BF16).astype(F32)
            total = pair if total is None else total + pair
        return split(total)

    if wraps < 2:
        pass_on(0)
    if chunks > 2:
        pass_on(1)
    for copy in cross_copies:
        copy.wait_recv()
    sums = []
    for c in range(chunks - 1):
        if 1 < c + 1 < chunks - 1:
            pass_on(c + 1)
        sums.append(pair_sum(c))
    if chunks > 1:
        pass_on(chunks - 1)
    local[2].wait()
    high = jnp.concatenate([h for h, _ in sums], axis=1)
    low = jnp.concatenate([l for _, l in sums], axis=1)
    for m in range(0, order, tile):
        rows = slice(m, m + tile)
        v = jnp.concatenate([take(vertex_v, (rows,), c) for c in range(chunks - 1)], axis=1)
        total_v[rows] = nt(v, high) + nt(v, low)
    high, low = pair_sum(chunks - 1)
    for m in range(0, order, tile):
        rows = slice(m, m + tile)
        v = take(vertex_v, (rows,), chunks - 1)
        total = total_v[rows] + nt(v, high) + nt(v, low)
        out[0, 0, rows] = (total / wraps).astype(BF16)

    for copy in seed_copies + pass_copies + cross_copies:
        copy.wait_send()


def per_device(rows_n, cols_n, seed_green, field_spins, hop_matrix, vertex):
    wraps = field_spins.shape[0]
    order, columns = seed_green.shape[2:]
    n_chunks = columns // 128
    dma = pltpu.SemaphoreType.DMA
    any_space = pl.BlockSpec(memory_space=pl.ANY)
    return pl.pallas_call(
        functools.partial(kernel, rows_n, cols_n),
        out_shape=jax.ShapeDtypeStruct(seed_green.shape, BF16),
        in_specs=[any_space] * 4,
        out_specs=pl.BlockSpec(memory_space=pltpu.VMEM),
        scratch_shapes=[
            pltpu.VMEM((order, columns), BF16),
            pltpu.VMEM((order, order), F32),
            pltpu.VMEM((order, order), BF16),
            pltpu.VMEM((wraps, 1, order), jnp.int32),
            pltpu.VMEM((order, order), BF16),
            pltpu.VMEM((order, order), BF16),
            pltpu.VMEM((order, order), BF16),
            pltpu.VMEM((wraps, columns, order), BF16),
            pltpu.VMEM((2, columns, order), BF16),
            pltpu.VMEM((wraps, order, columns), BF16),
            pltpu.VMEM((wraps, order, columns), BF16),
            pltpu.VMEM((wraps, columns, order), BF16),
            pltpu.VMEM((wraps, columns, order), BF16),
            pltpu.VMEM((order, columns), F32),
            dma((3,)),
            dma((n_chunks,)),
            dma((n_chunks,)),
            dma((n_chunks,)),
            dma((n_chunks,)),
            dma((wraps,)),
            dma((wraps,)),
            dma((2, wraps)),
            dma((2, wraps)),
        ],
        compiler_params=pltpu.CompilerParams(
            collective_id=0, has_side_effects=True, vmem_limit_bytes=62 * 1024 * 1024
        ),
    )(seed_green, field_spins, hop_matrix, vertex)


def solution(mesh):
    body = functools.partial(per_device, mesh.shape["rowt"], mesh.shape["colt"])
    return jax.shard_map(
        body,
        mesh=mesh,
        in_specs=(
            P(("groups", "rowt"), "colt", None, "site"),
            P(None, ("groups", "rowt"), None),
            P(),
            P(),
        ),
        out_specs=P(("groups", "rowt"), "colt", None, "site"),
        check_vma=False,
    )
```

time: 38 us -> 32.4 us (0.85)
  Pallas kernels: 35.9 us -> 30.3 us
    pallas_call x1, Pallas kernels: 35.9 us -> 30.3 us  [per_device(): pl.pallas_call(functools.partial(kernel, rows_n, cols_n), out_shape=jax.S...]
where the time goes in v2:
time: 32.4 us; the launch traced here: 32.2 us
  Pallas kernels  30.3 us (94%)
  local copies, waits for them, and re-layouts  1.94 us (6%)
    pallas_call x1, Pallas kernels, per_device(): pl.pallas_call(functools.partial(kernel, rows_n, cols_n), out_shape=jax.S...  30.3 us
    unnamed x1, local copies, waits for them, and re-layouts  1.94 us

profile of v2, /device:TPU:0, one launch (start us, length us, event | category | flops | bytes accessed | tf_op | source)
XLA Modules:
  0.0 32.2 jit_solution(14937047842613061687)
XLA Ops:
  0.0 30.3 %shard_map.46 = bf16[1,1,768,384]{3,2,1,0:T(8,128)(2,1)} custom-call(bf16[1,1,768,384]{3,2,1,0:T(8,128)(2,1)} %seed.1, s32[4,1,768]{2,1,0:T(1,128)} %spins.1, f32[768,768]{1,0:T(8,128)} %hop.1, bf16[768,768]{1,0:T(8,128)(2,1)} %vertex.1), custom_call_target="tpu_custom_call" | custom-call | tf_op jit(solution)/shard_map/pallas_call | solution.py:227
  30.3 1.9 %copy.6 = bf16[1,1,768,384]{3,2,1,0:T(8,128)(2,1)} copy(bf16[1,1,768,384]{3,2,1,0:T(8,128)(2,1)} %shard_map.46) | data formatting | bytes 1179648

commit v3 on v2

--- a/solution.py
+++ b/solution.py
@@ -126,7 +126,7 @@
         sign = jnp.where(lax.rem(row + w + 1, rows_n) == 0, F32(-1), F32(1))
         return sign * jnp.exp(coupling * (2.0 * spin_v[w].astype(F32) - 1.0))
 
-    tile = 256
+    tile = order
     cross_copies = []
     for w in range(wraps):
         products = []

time: 32.4 us -> 31.8 us (0.981)
  Pallas kernels: 30.3 us -> 29.7 us
    pallas_call x1, Pallas kernels: 30.3 us -> 29.7 us  [per_device(): pl.pallas_call(functools.partial(kernel, rows_n, cols_n), out_shape=jax.S...]
where the time goes in v3:
time: 31.8 us; the launch traced here: 31.7 us
  Pallas kernels  29.7 us (93%)
  local copies, waits for them, and re-layouts  1.94 us (6%)
    pallas_call x1, Pallas kernels, per_device(): pl.pallas_call(functools.partial(kernel, rows_n, cols_n), out_shape=jax.S...  29.7 us
    unnamed x1, local copies, waits for them, and re-layouts  1.94 us

profile of v3, /device:TPU:0, one launch (start us, length us, event | category | flops | bytes accessed | tf_op | source)
XLA Modules:
  0.0 31.7 jit_solution(9762509902023948205)
XLA Ops:
  0.0 29.7 %shard_map.46 = bf16[1,1,768,384]{3,2,1,0:T(8,128)(2,1)} custom-call(bf16[1,1,768,384]{3,2,1,0:T(8,128)(2,1)} %seed.1, s32[4,1,768]{2,1,0:T(1,128)} %spins.1, f32[768,768]{1,0:T(8,128)} %hop.1, bf16[768,768]{1,0:T(8,128)(2,1)} %vertex.1), custom_call_target="tpu_custom_call" | custom-call | tf_op jit(solution)/shard_map/pallas_call | solution.py:227
  29.7 1.9 %copy.6 = bf16[1,1,768,384]{3,2,1,0:T(8,128)(2,1)} copy(bf16[1,1,768,384]{3,2,1,0:T(8,128)(2,1)} %shard_map.46) | data formatting | bytes 1179648
